TPU v7x, 32 devices: a whole 2x2x4 slice. The times are simulated.
32 devices in a mesh: leaf: 8 (over z, y), layer: 4 (over x, core).
Axes of the slice: x: 2, y: 2, z: 4, core: 2. Of those that a mesh axis runs over, the one named last changes fastest.
Arguments:
- schur_blocks: float32 [8, 2048, 2048], P('leaf', 'layer'), as said below
Outputs:
- merged: float32 [8, 1536, 3072], P('leaf', 'layer')
- cousin_sum: float32 [8, 512, 512], P('leaf', 'layer')
Inputs may be any that keep to these rules, and one draw needn't show every extreme that they name: `schur_blocks`: symmetric and positive definite.
All inputs are finite; a program needn't handle non-finite values.
Results may differ from a plain program's by a relative error of at most 0.0001.
Values sent between devices are 32-bit elements; how exact they have to be, the bound alone decides.
A program may use at most 64 MiB of HBM per device.

v0:
```python
import jax
import jax.numpy as jnp
from jax import lax
from jax.sharding import PartitionSpec as P

SEP = 512
SHARED = 512


def partner(value, axis, stride):
    mask = 2**stride
    pairs = [(source, source ^ mask) for source in range(lax.axis_size(axis))]
    return lax.ppermute(value, axis, pairs)


def on_device(schur_blocks):
    highest = lax.Precision.HIGHEST
    layers = lax.axis_size("layer")
    local = schur_blocks[0]
    slab = local.shape[0]
    width = local.shape[1]
    sep_slab = SEP // layers
    outer_slab = slab - sep_slab
    shared_slab = SHARED // layers
    outer_all = width - SEP
    split_cols = local.reshape(slab, layers, slab)
    sep_cols = split_cols[:, :, :sep_slab].reshape(slab, SEP)
    out_cols = split_cols[:, :, sep_slab:].reshape(slab, outer_all)
    own_sep = sep_cols[:sep_slab]
    sibling = partner(own_sep, "leaf", 0)
    sepmat = lax.all_gather(own_sep + sibling, "layer", axis=0, tiled=True)
    lower = jnp.linalg.cholesky(sepmat)
    coupling = sep_cols[sep_slab:]
    factor_own = lax.linalg.triangular_solve(lower, coupling.T, left_side=True, lower=True)
    parity = lax.axis_index("leaf") % 2
    selector = (jnp.arange(2) == parity).astype(jnp.float32)
    direct_rows = out_cols[sep_slab:]
    gathered = lax.all_gather(factor_own, "layer", axis=1, tiled=True)
    far_factor = partner(gathered, "leaf", 0)
    low_first = jnp.stack([gathered, far_factor])
    high_first = jnp.stack([far_factor, gathered])
    paired = jnp.where(parity == 0, low_first, high_first)
    product = jnp.einsum(
        "pr,kpc->rkc", factor_own, paired, precision=highest, preferred_element_type=jnp.float32
    )
    merged_rows = direct_rows[:, None, :] * selector[None, :, None] - product
    merged = merged_rows.reshape(outer_slab, 2 * outer_all)
    grouped = merged_rows.reshape(outer_slab, 2, layers, outer_slab)[:shared_slab]
    own_block = jnp.where(parity == 0, grouped[:, 0], grouped[:, 1])
    own_shared = own_block[:, :, :shared_slab].reshape(shared_slab, SHARED)
    cousin = partner(own_shared, "leaf", 1)
    cousin_sum = own_shared + cousin
    return (merged[None], cousin_sum[None])


def solution(mesh):
    placed = (P("leaf", "layer", None),)
    return jax.shard_map(
        on_device,
        mesh=mesh,
        in_specs=placed,
        out_specs=(P("leaf", "layer", None), P("leaf", "layer", None)),
        check_vma=False,
    )
```

profile of v0, /device:TPU:0, one launch (start us, length us, event | category | flops | bytes accessed | tf_op | source)
XLA Modules:
  0.0 329.5 jit_solution(8264649815688470065)
XLA Ops:
  7.2 6.0 %reshape_squeeze.3 = f32[512,4,512]{2,1,0:T(4,128)} reshape(f32[1,512,2048]{2,1,0:T(8,128)} %param.1) | data formatting | bytes 8388608 | tf_op jit(solution)/shard_map/reshape;squeeze | solution.py:26
  13.2 1.0 slice.161
  14.3 3.0 collective-permute-start
  17.4 6.3 %collective-permute-done = f32[128,512]{0,1:T(8,128)S(1)} collective-permute-done((f32[128,512]{0,1:T(8,128)S(1)}, f32[128,512]{0,1:T(8,128)S(1)}, u32[]{:S(2)}, u32[]{:S(2)}) %collective-permute-start) | collective-permute-done | bytes 262176 | tf_op jit(solution)/shard_map/ppermute | solution.py:13
  24.5 1.2 slice.162
  25.8 17.1 %all-gather.3.cloned.1.call-done = f32[512,512]{0,1:T(8,128)} async-done(((f32[128,512]{0,1:T(8,128)}), f32[512,512]{0,1:T(8,128)}) %all-gather.3.cloned.1.call-update) | async-done | bytes 1048592 | tf_op jit(solution)/shard_map/all_gather | solution.py:31
  42.9 1.6 copy.7
  44.5 1.4 fusion.7
  45.9 11.7 %cholesky.104 = f32[128,128]{1,0:T(8,128)S(1)} custom-call(f32[128,128]{1,0:T(8,128)S(1)} %cholesky.266), custom_call_target="Cholesky" | custom-call | tf_op jit(solution)/shard_map/jit(cholesky)/cholesky | solution.py:32
  57.7 9.8 %custom-call.30 = f32[1,128,128]{1,2,0:T(8,128)S(1)} custom-call(f32[1,128,128]{2,1,0:T(8,128)S(1)} %get-tuple-element.31), custom_call_target="InvertDiagBlocksLowerTriangular" | custom-call | tf_op jit(solution)/shard_map/jit(cholesky)/cholesky | solution.py:32
  68.3 11.7 %cholesky.217 = f32[128,128]{1,0:T(8,128)S(1)} custom-call(f32[128,128]{1,0:T(8,128)S(1)} %cholesky.270), custom_call_target="Cholesky" | custom-call | tf_op jit(solution)/shard_map/jit(cholesky)/cholesky | solution.py:32
  80.0 10.0 %custom-call.31 = f32[1,128,128]{1,2,0:T(8,128)S(1)} custom-call(f32[1,128,128]{2,1,0:T(8,128)S(1)} %get-tuple-element.28), custom_call_target="InvertDiagBlocksLowerTriangular" | custom-call | tf_op jit(solution)/shard_map/jit(cholesky)/cholesky | solution.py:32
  90.7 11.7 %cholesky.238 = f32[128,128]{1,0:T(8,128)S(1)} custom-call(f32[128,128]{1,0:T(8,128)S(1)} %cholesky.275), custom_call_target="Cholesky" | custom-call | tf_op jit(solution)/shard_map/jit(cholesky)/cholesky | solution.py:32
  103.2 9.8 %custom-call.32 = f32[1,128,128]{1,2,0:T(8,128)S(1)} custom-call(f32[1,128,128]{2,1,0:T(8,128)S(1)} %get-tuple-element.25), custom_call_target="InvertDiagBlocksLowerTriangular" | custom-call | tf_op jit(solution)/shard_map/jit(cholesky)/cholesky | solution.py:32
  113.6 11.7 %cholesky.255 = f32[128,128]{1,0:T(8,128)S(1)} custom-call(f32[128,128]{1,0:T(8,128)S(1)} %convolution_subtract_fusion.5), custom_call_target="Cholesky" | custom-call | tf_op jit(solution)/shard_map/jit(cholesky)/cholesky | solution.py:32
  126.0 10.9 %compare_reduce_fusion.2 = (pred[]{:T(512)}, pred[]{:T(512)}) fusion(f32[128]{0:T(128)S(1)} %get-tuple-element.27, f32[128]{0:T(128)S(1)} %get-tuple-element.30), kind=kLoop, calls=%fused_computation.72 | loop fusion | flops 510 | bytes 1026 | tf_op jit(solution)/shard_map/jit(cholesky)/cholesky | solution.py:32
  139.6 8.5 %while.1 = (s32[]{:T(128)}, f32[512,512]{1,0:T(8,128)S(1)}, s32[4,2]{0,1:T(2,128)S(1)}, f32[4,128,128]{2,1,0:T(8,128)S(1)}, s32[]{:T(128)}) while((s32[]{:T(128)}, f32[512,512]{1,0:T(8,128)S(1)}, s32[4,2]{0,1:T(2,128)S(1)}, f32[4,128,128]{2,1,0:T(8,128)S(1)}, s32[]{:T(128)}) %tuple.32), condition=%wide.while_cond, body=%wide.while_body.sunk | while | flops 2 | bytes 131189 | solution.py:34
  140.3 1.4 bitcast_dynamic-update-slice_fusion.2
  142.4 1.4 bitcast_dynamic-update-slice_fusion.2
  144.5 1.4 bitcast_dynamic-update-slice_fusion.2
  146.7 1.4 bitcast_dynamic-update-slice_fusion.2
  148.1 39.3 %custom-call.33 = f32[4,128,128]{1,2,0:T(8,128)S(1)} custom-call(f32[4,128,128]{2,1,0:T(8,128)S(1)} %get-tuple-element.9), custom_call_target="InvertDiagBlocksLowerTriangular" | custom-call | tf_op jit(solution)/shard_map/triangular_solve | solution.py:34
  190.0 2.0 convolution_subtract_fusion
  193.4 28.7 %all-gather.5.cloned.1.call-done = f32[512,1536]{1,0:T(8,128)} async-done(((f32[512,384]{1,0:T(8,128)}), f32[512,1536]{1,0:T(8,128)}) %all-gather.5.cloned.1.call-update) | async-done | bytes 3145744 | tf_op jit(solution)/shard_map/all_gather | solution.py:38
  222.1 1.5 collective-permute-start.1
  223.6 2.1 slice.160
  225.8 66.8 %collective-permute-done.1 = f32[512,1536]{1,0:T(8,128)} collective-permute-done((f32[512,1536]{1,0:T(8,128)}, f32[512,1536]{1,0:T(8,128)}, u32[]{:S(2)}, u32[]{:S(2)}) %collective-permute-start.1) | collective-permute-done | bytes 3145760 | tf_op jit(solution)/shard_map/ppermute | solution.py:13
  292.7 12.2 %multiply_subtract_fusion = f32[384,2,1536]{2,0,1:T(8,128)S(1)} fusion(f32[1,512,1536]{2,1,0:T(8,128)} %bitcast.15, f32[1,512,1536]{2,1,0:T(8,128)S(1)} %bitcast.80, pred[]{:T(512)S(6)} %eq.18, f32[2]{0:T(128)S(1)} %compare_convert_fusion, f32[384,1536]{1,0:T(8,128)S(1)} %bitcast.77, f32[128,384]{1,0:T(8,128)S(1)} %fusion.28, f32[128,384]{1,0:T(8,128)S(1)} %fusion.29, ...), kind=kOutput, calls=%fused_computation.9 | convolution fusion | flops 7255425024 | bytes 14155785 | tf_op jit(solution)/shard_map/pr,kpc->rkc/dot_general | solution.py:43
  304.9 2.2 copy-done
  308.0 1.6 collective-permute-start.2
  309.6 6.1 %copy.9 = f32[384,2,1536]{0,2,1:T(8,128)} copy(f32[384,2,1536]{2,0,1:T(8,128)} %copy-done) | data formatting | bytes 9437184 | tf_op jit(solution)/shard_map/sub | solution.py:46
  315.7 6.0 %copy.10 = f32[1,384,3072]{2,1,0:T(8,128)} copy(f32[1,384,3072]{1,2,0:T(8,128)} %bitcast.78) | data formatting | bytes 9437184
  (56 shorter events, 13.0 us)
Async XLA Ops:
  7.2 35.7 %all-gather.3.cloned.1.call-start = ((), (), s32[]{:S(2)}) async-start(), calls=%async_computation | async-start | bytes 1310720 | tf_op jit(solution)/shard_map/all_gather | solution.py:31
  14.3 9.3 %collective-permute-start = (f32[128,512]{0,1:T(8,128)S(1)}, f32[128,512]{0,1:T(8,128)S(1)}, u32[]{:S(2)}, u32[]{:S(2)}) collective-permute-start(f32[128,512]{0,1:T(8,128)S(1)} %bitcast.88), channel_id=1, source_target_pairs={{0,4},{4,0},{8,12},{12,8},{16,20},{20,16},{24,28},{28,24},{1,5},{5... | collective-permute-start | bytes 786440 | tf_op jit(solution)/shard_map/ppermute | solution.py:13
  24.4 197.7 %all-gather.5.cloned.1.call-start = ((), (), s32[]{:S(2)}) async-start(), calls=%async_computation.1 | async-start | bytes 3932160 | tf_op jit(solution)/shard_map/all_gather | solution.py:38
  148.1 40.7 %copy-start.2 = (f32[512,512]{1,0:T(8,128)}, f32[512,512]{1,0:T(8,128)S(1)}, u32[]{:S(2)}) copy-start(f32[512,512]{1,0:T(8,128)S(1)} %get-tuple-element.87) | copy-start | bytes 3145732
  222.1 70.6 %collective-permute-start.1 = (f32[512,1536]{1,0:T(8,128)}, f32[512,1536]{1,0:T(8,128)}, u32[]{:S(2)}, u32[]{:S(2)}) collective-permute-start(f32[512,1536]{1,0:T(8,128)} %all-gather.5.cloned.1.call-done), channel_id=1, source_target_pairs={{0,4},{4,0},{8,12},{12,8},{16,20},{20,16},{24,28},{28,24},{1,5},{5... | collective-permute-start | bytes 9437192 | tf_op jit(solution)/shard_map/ppermute | solution.py:13
  225.6 67.0 %copy-start.1 = (f32[512,1536]{1,0:T(8,128)S(1)}, f32[512,1536]{1,0:T(8,128)}, u32[]{:S(2)}) copy-start(f32[512,1536]{1,0:T(8,128)} %all-gather.5.cloned.1.call-done) | copy-start | bytes 9437188
  304.9 2.2 copy-start
  308.0 13.7 %collective-permute-start.2 = (f32[128,512]{1,0:T(8,128)S(1)}, f32[128,512]{1,0:T(8,128)S(1)}, u32[]{:S(2)}, u32[]{:S(2)}) collective-permute-start(f32[128,512]{1,0:T(8,128)S(1)} %bitcast.89), channel_id=1, source_target_pairs={{0,8},{4,12},{8,0},{12,4},{16,24},{20,28},{24,16},{28,20},{1,9},{5... | collective-permute-start | bytes 786440 | tf_op jit(solution)/shard_map/ppermute | solution.py:13
Sparse Core Ops, SparseCore 0:
  24.6 18.3 all-gather.2
  193.5 28.5 all-gather.4
where the time goes:
time: 334 us; the launch traced here: 330 us
  other arithmetic  132 us (40%)
  waiting for transfers between devices  119 us (36%)
  local copies, waits for them, and re-layouts  35.7 us (11%)
  matrix products  19 us (6%)
  between operations  17.1 us (5%)
  starting transfers between devices  6.14 us (2%)
    another operation x14, other arithmetic, on_device(): lower = jnp.linalg.cholesky(sepmat)  88.9 us
    ppermute x3, waiting for transfers between devices, partner(): return lax.ppermute(value, axis, pairs)  73.1 us
    another operation x4, other arithmetic, on_device(): lax.linalg.triangular_solve(lower, coupling.T, left_side=True, lower=True)  40.4 us
    all_gather x1, waiting for transfers between devices, on_device(): gathered = lax.all_gather(factor_own, 'layer', axis=1, tiled=True)  28.7 us
    all_gather x1, waiting for transfers between devices, on_device(): sepmat = lax.all_gather(own_sep + sibling, 'layer', axis=0, tiled=True)  17.1 us
    dot_general x1, matrix products, on_device(): jnp.einsum('pr,kpc->rkc', factor_own, paired, precision=highest, preferre...  12.2 us
    unnamed x11, local copies, waits for them, and re-layouts  8.59 us
    another operation x12, local copies, waits for them, and re-layouts  8.39 us
  transfers between devices with their start and end apart: 5, of which 4 were waited for; matrix products, arithmetic and copies ran while one was open for 5% of the time, Pallas kernels for 0%

commit v1 on v0

v1 whole, which is shorter than its diff:
```python
import functools

import jax
import jax.numpy as jnp
from jax import lax
from jax.experimental import pallas as pl
from jax.experimental.pallas import tpu as pltpu
from jax.sharding import PartitionSpec as P

MESH = pl.DeviceIdType.MESH
F32 = jnp.float32
BF16 = jnp.bfloat16
W = 8
CORE, ACROSS, SIBLING = 1, 2, 4


def dot32(a, b, dims=((1,), (0,))):
    return lax.dot_general(
        a, b, (dims, ((), ())), precision=lax.Precision.HIGHEST, preferred_element_type=F32
    )


def split(a):
    high = a.astype(BF16)
    low = (a - high.astype(F32)).astype(BF16)
    return high, low


def invert_block(a_ref):
    n = a_ref.shape[0]
    lane = lax.broadcasted_iota(jnp.int32, (W, n), 1)
    row = lax.broadcasted_iota(jnp.int32, (W, n), 0)
    lane_all = lax.broadcasted_iota(jnp.int32, (n, n), 1)

    def panel(p, carry):
        rows = pl.ds(pl.multiple_of(p * W, W), W)
        strip = a_ref[rows, :]
        cols = [jnp.broadcast_to(strip[:, j : j + 1], (W, n)) for j in range(W)]
        rest = jnp.where(lane < W, jnp.where(lane == row, 1.0, 0.0), strip)
        for k in range(W):
            inv = 1.0 / jnp.broadcast_to(cols[k][k : k + 1, :], (W, n))
            pivot = row == k
            weight = cols[k]

            def clear(v):
                scaled = jnp.broadcast_to(v[k : k + 1, :], (W, n)) * inv
                return jnp.where(pivot, scaled, v - weight * scaled)

            rest = clear(rest)
            for j in range(k + 1, W):
                cols[j] = clear(cols[j])
        whole = a_ref[...]
        update = jnp.where(lane_all < W, 0.0, whole)
        for j in range(W):
            update = update - whole[:, j : j + 1] * rest[j : j + 1, :]
        a_ref[...] = pltpu.roll(update, n - W, 1)
        a_ref[rows, :] = pltpu.roll(rest, n - W, 1)
        return carry

    lax.fori_loop(0, n // W, panel, 0)


def gather_kernel(
    layers, a_ref, blocks_ref, y_ref, shared_ref,
    sep, mat, diag, mine, near, direct, send_sem, recv_sem, local_sem,
):
    leaf = lax.axis_index("leaf")
    layer = lax.axis_index("layer")
    core = lax.rem(layer, 2)
    slab = a_ref.shape[0]
    ps = sep.shape[1]
    outer = slab - ps
    sh = shared_ref.shape[0]
    chunks = outer // ps

    def flip(value, bit):
        return value + bit - 2 * bit * lax.rem(value // bit, 2)

    targets = {
        CORE: (leaf, flip(layer, 1)),
        ACROSS: (leaf, flip(layer, 2)),
        SIBLING: (flip(leaf, 1), layer),
    }
    corner = (
        jnp.where(core == 0, flip(leaf, 1), leaf),
        jnp.where(core == 0, layer, flip(layer, 2)),
    )

    barrier = pltpu.get_barrier_semaphore()
    for target in targets.values():
        pl.semaphore_signal(barrier, inc=1, device_id=target, device_id_type=MESH)

    loads = []
    for h in range(layers):
        cols = pl.ds(h * slab, ps)
        into = pl.ds(h * ps, ps)
        loads.append(pltpu.make_async_copy(
            a_ref.at[pl.ds(0, ps), cols], sep.at[0, :, into], local_sem.at[h]))
    for h in range(layers):
        cols = pl.ds(h * slab, ps)
        into = pl.ds(h * ps, ps)
        loads.append(pltpu.make_async_copy(
            a_ref.at[pl.ds(ps, outer), cols], mine.at[:, into], local_sem.at[layers + h]))
    for h in range(layers):
        loads.append(pltpu.make_async_copy(
            a_ref.at[pl.ds(ps, sh), pl.ds(h * slab + ps, sh)],
            direct.at[:, pl.ds(h * sh, sh)], local_sem.at[2 * layers + h]))
    for load in loads:
        load.start()

    def place(slot, q):
        if q == 0:
            return sep.at[slot]
        return blocks_ref.at[slot, pl.ds((q - 1) * ps, ps), :]

    def origin(slot, q):
        if q > 0 and isinstance(slot, int) and slot == 0:
            return mine.at[pl.ds((q - 1) * ps, ps), :]
        return place(slot, q)

    sources = {1: 0, 2: 0, 4: 0, 3: 2, 5: 4, 6: 2 + 2 * core, 7: 6}
    ways = {1: CORE, 2: ACROSS, 4: SIBLING, 3: CORE, 5: CORE, 7: CORE}

    def transfer(slot, q):
        return pltpu.make_async_remote_copy(
            src_ref=origin(sources[slot], q),
            dst_ref=place(slot, q),
            send_sem=send_sem.at[slot, q],
            recv_sem=recv_sem.at[slot, q],
            device_id=corner if slot == 6 else targets[ways[slot]],
            device_id_type=MESH,
        )

    def first(q):
        for slot in (SIBLING, ACROSS, CORE):
            transfer(slot, q).start()

    def second(q):
        transfer(2, q).wait_recv()
        transfer(4, q).wait_recv()
        transfer(6, q).start()
        transfer(3, q).start()
        transfer(5, q).start()

    def third(q):
        transfer(6, q).wait_recv()
        transfer(7, q).start()

    def last(q):
        for slot in (1, 3, 5, 7):
            transfer(slot, q).wait_recv()

    for load in loads[:layers]:
        load.wait()
    pl.semaphore_wait(barrier, 3)
    first(0)
    for load in loads[layers:]:
        load.wait()
    keep = pltpu.make_async_copy(mine, blocks_ref.at[0], local_sem.at[3 * layers])
    keep.start()
    second(0)
    first(1)
    third(0)
    for q in range(2, chunks + 1):
        first(q)
    last(0)

    for r in range(layers):
        h = layer + r - 2 * (
            lax.rem(layer, 2) * (r % 2) + 2 * lax.rem(layer // 2, 2) * (r // 2)
        )
        mat[pl.ds(pl.multiple_of(h * ps, ps), ps), :] = sep[r] + sep[r + SIBLING]

    for b in range(layers):
        mid = slice(b * ps, (b + 1) * ps)
        diag[...] = mat[mid, mid]
        invert_block(diag)
        turned = dot32(diag[...], mat[mid, :])
        mat[mid, :] = turned
        mat[mid, mid] = diag[...]
        turned = mat[mid, :]
        for other in range(layers):
            if other == b:
                continue
            rows = slice(other * ps, (other + 1) * ps)
            weight = mat[rows, mid]
            mat[rows, mid] = jnp.zeros((ps, ps), F32)
            mat[rows, :] = mat[rows, :] - dot32(weight, turned)
        if b + 1 <= chunks:
            second(b + 1)
        if 1 <= b <= chunks:
            third(b)
    for q in range(layers, chunks + 1):
        third(q)
    last(1)
    fetch = [
        pltpu.make_async_copy(blocks_ref.at[r, pl.ds(0, sh), :], near.at[r - 1], local_sem.at[r])
        for r in range(1, layers)
    ]
    for copy in fetch:
        copy.start()
    y_ref[...] = dot32(mine[...], mat[...])
    for copy in fetch:
        copy.wait()
    for r in range(layers):
        h = layer + r - 2 * (
            lax.rem(layer, 2) * (r % 2) + 2 * lax.rem(layer // 2, 2) * (r // 2)
        )
        cols = pl.ds(pl.multiple_of(h * sh, sh), sh)
        far = mine[0:sh, :] if r == 0 else near[r - 1]
        shared_ref[:, cols] = direct[:, cols] - dot32(y_ref[0:sh, :], far, ((1,), (1,)))
    keep.wait()
    for q in range(2, chunks + 1):
        last(q)
    for q in range(chunks + 1):
        for slot in range(1, 8):
            transfer(slot, q).wait_send()


def merge_kernel(layers, where_ref, y_ref, block_ref, a_ref, out_ref, wide):
    r = pl.program_id(0)
    depth = y_ref.shape[1]
    ps = a_ref.shape[0] - out_ref.shape[0]

    @pl.when(r == 0)
    def _():
        high, low = split(y_ref[...])
        wide[:, 0:depth] = high
        wide[:, depth : 2 * depth] = high
        wide[:, 2 * depth : 3 * depth] = low

    high, low = split(block_ref[0])
    far = jnp.concatenate([high, low, high], axis=1)
    product = lax.dot_general(
        wide[...], far, (((1,), (1,)), ((), ())), preferred_element_type=F32
    )

    @pl.when(r < layers)
    def _():
        out_ref[...] = a_ref[ps:, ps:] - product

    @pl.when(r >= layers)
    def _():
        out_ref[...] = 0.0 - product


def on_device(layers, schur_blocks):
    local = schur_blocks[0]
    slab, width = local.shape
    ps = slab // 4
    depth = layers * ps
    outer = slab - ps
    sh = ps
    group = 2 * layers
    chunks = outer // ps
    blocks, y, own = pl.pallas_call(
        functools.partial(gather_kernel, layers),
        out_shape=(
            jax.ShapeDtypeStruct((group, outer, depth), F32),
            jax.ShapeDtypeStruct((outer, depth), F32),
            jax.ShapeDtypeStruct((sh, layers * sh), F32),
        ),
        in_specs=[pl.BlockSpec(memory_space=pl.ANY)],
        out_specs=(
            pl.BlockSpec(memory_space=pl.ANY),
            pl.BlockSpec(memory_space=pltpu.VMEM),
            pl.BlockSpec(memory_space=pltpu.VMEM),
        ),
        scratch_shapes=[
            pltpu.VMEM((group, ps, depth), F32),
            pltpu.VMEM((depth, depth), F32),
            pltpu.VMEM((ps, ps), F32),
            pltpu.VMEM((outer, depth), F32),
            pltpu.VMEM((layers - 1, sh, depth), F32),
            pltpu.VMEM((sh, layers * sh), F32),
            pltpu.SemaphoreType.DMA((group, chunks + 1)),
            pltpu.SemaphoreType.DMA((group, chunks + 1)),
            pltpu.SemaphoreType.DMA((3 * layers + 1,)),
        ],
        compiler_params=pltpu.CompilerParams(
            collective_id=0, has_side_effects=True, vmem_limit_bytes=40 * 2**20
        ),
    )(local)

    leaf = lax.axis_index("leaf")
    layer = lax.axis_index("layer")
    me = (leaf % 2) * layers + layer
    order = jnp.bitwise_xor(me, jnp.arange(group, dtype=jnp.int32))
    slabs = jnp.bitwise_xor(layer, jnp.minimum(jnp.arange(group, dtype=jnp.int32), layers - 1))
    where = jnp.concatenate([order, slabs]).astype(jnp.int32)
    merged = pl.pallas_call(
        functools.partial(merge_kernel, layers),
        out_shape=jax.ShapeDtypeStruct((outer, group * outer), F32),
        grid_spec=pltpu.PrefetchScalarGridSpec(
            num_scalar_prefetch=1,
            grid=(group,),
            in_specs=[
                pl.BlockSpec((outer, depth), lambda r, w: (0, 0)),
                pl.BlockSpec((1, outer, depth), lambda r, w: (r, 0, 0)),
                pl.BlockSpec((slab, slab), lambda r, w: (0, w[group + r])),
            ],
            out_specs=pl.BlockSpec((outer, outer), lambda r, w: (0, w[r])),
            scratch_shapes=[pltpu.VMEM((outer, 3 * depth), BF16)],
        ),
        compiler_params=pltpu.CompilerParams(vmem_limit_bytes=40 * 2**20),
        cost_estimate=pl.CostEstimate(
            flops=6 * outer * depth * group * outer,
            bytes_accessed=4 * (group * outer * (outer + depth) + slab * width),
            transcendentals=0,
        ),
    )(where, y, blocks, local)
    count = lax.axis_size("leaf")
    cousin = lax.ppermute(own, "leaf", [(s, s ^ 2) for s in range(count)])
    return (merged[None], (own + cousin)[None])


def solution(mesh):
    placed = (P("leaf", "layer", None),)
    return jax.shard_map(
        functools.partial(on_device, mesh.shape["layer"]),
        mesh=mesh,
        in_specs=placed,
        out_specs=(P("leaf", "layer", None), P("leaf", "layer", None)),
        check_vma=False,
    )
```

time: 334 us -> 71.9 us (0.22); the launches traced: 330 us -> 71.7 us
  other arithmetic: 132 us -> 0.82 us
  waiting for transfers between devices: 119 us -> 0.01 us
  Pallas kernels: 0 us -> 58.8 us
  local copies, waits for them, and re-layouts: 35.7 us -> 9.81 us
  matrix products: 19 us -> 0 us
  between operations: 17.1 us -> 0.66 us
  starting transfers between devices: 6.14 us -> 1.59 us
    another operation x18 -> x0, other arithmetic: 129 us -> none  [the longest x14 88.9 us: on_device(): lower = jnp.linalg.cholesky(sepmat)]
    ppermute x3 -> x1, waiting for transfers between devices: 73.1 us -> 0.01 us  [on_device(): cousin = lax.ppermute(own, 'leaf', [(s, s ^ 2) for s in range(count)])]
    pallas_call x0 -> x2, Pallas kernels: none -> 58.8 us  [the longest x1 50 us: on_device(): pl.pallas_call(functools.partial(gather_kernel, layers), out_shape=(jax.S...]
    all_gather x2 -> x0, waiting for transfers between devices: 45.8 us -> none  [the longest x1 28.7 us: on_device(): gathered = lax.all_gather(factor_own, 'layer', axis=1, tiled=True)]
    another operation x18 -> x0, local copies, waits for them, and re-layouts: 14.6 us -> none
    dot_general x1 -> x0, matrix products: 12.2 us -> none  [on_device(): jnp.einsum('pr,kpc->rkc', factor_own, paired, precision=highest, preferre...]
    another operation x13 -> x0, matrix products: 6.79 us -> none  [the longest x7 4.93 us: on_device(): lax.linalg.triangular_solve(lower, coupling.T, left_side=True, lower=True)]
    sub x1 -> x0, local copies, waits for them, and re-layouts: 6.06 us -> none  [on_device(): merged_rows = direct_rows[:, None, :] * selector[None, :, None] - product]
  transfers between devices with their start and end apart: 5 -> 1, of which waited for: 4 -> 0; matrix products, arithmetic and copies ran while one was open for 5% -> 0% of each run, Pallas kernels for 0% -> 12%
where the time goes in v1:
time: 71.9 us; the launch traced here: 71.7 us
  Pallas kernels  58.8 us (82%)
  local copies, waits for them, and re-layouts  9.81 us (14%)
  starting transfers between devices  1.59 us (2%)
  other arithmetic  0.82 us (1%)
    pallas_call x1, Pallas kernels, on_device(): pl.pallas_call(functools.partial(gather_kernel, layers), out_shape=(jax.S...  50 us
    unnamed x8, local copies, waits for them, and re-layouts  9.81 us
    pallas_call x1, Pallas kernels, on_device(): pl.pallas_call(functools.partial(merge_kernel, layers), out_shape=jax.Sha...  8.8 us
    ppermute x1, starting transfers between devices, on_device(): cousin = lax.ppermute(own, 'leaf', [(s, s ^ 2) for s in range(count)])  1.59 us
  transfers between devices with their start and end apart: 1, of which 0 were waited for; matrix products, arithmetic and copies ran while one was open for 0% of the time, Pallas kernels for 12%

profile of v1, /device:TPU:0, one launch (start us, length us, event | category | flops | bytes accessed | tf_op | source)
XLA Modules:
  0.0 71.7 jit_solution(7991621565055425101)
XLA Ops:
  0.6 0.0 copy-start
  0.6 2.2 %copy-done = f32[1,512,2048]{2,1,0:T(8,128)S(1)} copy-done((f32[1,512,2048]{2,1,0:T(8,128)S(1)}, f32[1,512,2048]{2,1,0:T(8,128)}, u32[]{:S(2)}) %copy-start) | copy-done | bytes 4194328
  2.8 50.0 %shard_map.30 = (f32[8,384,512]{2,1,0:T(8,128)S(1)}, f32[384,512]{1,0:T(8,128)S(1)}, f32[128,512]{1,0:T(8,128)S(1)}) custom-call(f32[512,2048]{1,0:T(8,128)S(1)} %bitcast.4), custom_call_target="tpu_custom_call" | custom-call | tf_op jit(solution)/shard_map/pallas_call | solution.py:256
  52.8 0.0 copy-start.2
  52.9 2.7 %copy-done.2 = f32[8,384,512]{2,1,0:T(8,128)} copy-done((f32[8,384,512]{2,1,0:T(8,128)}, f32[8,384,512]{2,1,0:T(8,128)S(1)}, u32[]{:S(2)}) %copy-start.2) | copy-done | bytes 6291480
  55.5 1.6 %collective-permute-start = (f32[128,512]{1,0:T(8,128)S(1)}, f32[128,512]{1,0:T(8,128)S(1)}, u32[]{:S(2)}, u32[]{:S(2)}) collective-permute-start(f32[128,512]{1,0:T(8,128)S(1)} %get-tuple-element.7), channel_id=1, source_target_pairs={{0,8},{4,12},{8,0},{12,4},{16,24},{20,28},{24,16},{28,20},{1,9},{5... | collective-permute-start | bytes 786440 | tf_op jit(solution)/shard_map/ppermute | solution.py:313
  57.1 0.1 pad_add_fusion.where_ref
  57.2 0.0 copy-start.1
  57.2 2.2 %copy-done.1 = f32[1,512,2048]{2,1,0:T(8,128)S(1)} copy-done((f32[1,512,2048]{2,1,0:T(8,128)S(1)}, f32[1,512,2048]{2,1,0:T(8,128)}, u32[]{:S(2)}) %copy-start.1) | copy-done | bytes 4194328
  59.4 0.0 copy-start.3
  59.4 2.8 %copy-done.3 = f32[8,384,512]{2,1,0:T(8,128)S(1)} copy-done((f32[8,384,512]{2,1,0:T(8,128)S(1)}, f32[8,384,512]{2,1,0:T(8,128)}, u32[]{:S(2)}) %copy-start.3) | copy-done | bytes 6291480
  62.2 8.8 %shard_map.31 = f32[384,3072]{1,0:T(8,128)} custom-call(s32[16]{0:T(128)S(1)} %pad_add_fusion.where_ref, f32[384,512]{1,0:T(8,128)S(1)} %get-tuple-element.5.y_ref, f32[8,384,512]{2,1,0:T(8,128)S(1)} %copy-done.3, f32[512,2048]{1,0:T(8,128)S(1)} %bitcast.5), custom_call_target="tpu_custom_call" | custom-call | flops 3623878656 | bytes 15204352 | tf_op jit(solution)/shard_map/pallas_call | solution.py:291
  71.0 0.0 collective-permute-done
  71.0 0.7 %add_bitcast_fusion = f32[1,128,512]{2,1,0:T(8,128)} fusion(f32[128,512]{1,0:T(8,128)S(1)} %get-tuple-element.7, f32[128,512]{1,0:T(8,128)S(1)} %collective-permute-done), kind=kLoop, calls=%fused_computation | loop fusion | flops 65536 | bytes 786432 | tf_op jit(solution)/shard_map/broadcast_in_dim | solution.py:314
  (1 shorter events, 0.0 us)
Async XLA Ops:
  0.6 2.2 %copy-start = (f32[1,512,2048]{2,1,0:T(8,128)S(1)}, f32[1,512,2048]{2,1,0:T(8,128)}, u32[]{:S(2)}) copy-start(f32[1,512,2048]{2,1,0:T(8,128)} %param.1) | copy-start | bytes 12582916
  52.8 2.7 %copy-start.2 = (f32[8,384,512]{2,1,0:T(8,128)}, f32[8,384,512]{2,1,0:T(8,128)S(1)}, u32[]{:S(2)}) copy-start(f32[8,384,512]{2,1,0:T(8,128)S(1)} %get-tuple-element.6.block_ref) | copy-start | bytes 18874372
  55.5 15.4 %collective-permute-start = (f32[128,512]{1,0:T(8,128)S(1)}, f32[128,512]{1,0:T(8,128)S(1)}, u32[]{:S(2)}, u32[]{:S(2)}) collective-permute-start(f32[128,512]{1,0:T(8,128)S(1)} %get-tuple-element.7), channel_id=1, source_target_pairs={{0,8},{4,12},{8,0},{12,4},{16,24},{20,28},{24,16},{28,20},{1,9},{5... | collective-permute-start | bytes 786440 | tf_op jit(solution)/shard_map/ppermute | solution.py:313
  57.2 2.2 %copy-start.1 = (f32[1,512,2048]{2,1,0:T(8,128)S(1)}, f32[1,512,2048]{2,1,0:T(8,128)}, u32[]{:S(2)}) copy-start(f32[1,512,2048]{2,1,0:T(8,128)} %param.1) | copy-start | bytes 12582916
  59.4 2.8 %copy-start.3 = (f32[8,384,512]{2,1,0:T(8,128)S(1)}, f32[8,384,512]{2,1,0:T(8,128)}, u32[]{:S(2)}) copy-start(f32[8,384,512]{2,1,0:T(8,128)} %copy-done.2) | copy-start | bytes 18874372

commit v2 on v1

--- a/solution.py
+++ b/solution.py
@@ -26,43 +26,70 @@
     return high, low
 
 
-def invert_block(a_ref):
-    n = a_ref.shape[0]
+def refine(d):
+    r = pl.reciprocal(d, approx=True)
+    r = r * (2.0 - d * r)
+    return r * (2.0 - d * r)
+
+
+def rank_update(old, pivots):
+    lane = lax.broadcasted_iota(jnp.int32, old.shape, 1)
+    terms = [old[:, j : j + 1] * pivots[j : j + 1, :] for j in range(W)]
+    while len(terms) > 1:
+        terms = [terms[i] + terms[i + 1] for i in range(0, len(terms), 2)]
+    return jnp.where(lane < W, 0.0, old) - terms[0]
+
+
+def pivot_rows(strip, first):
+    n = strip.shape[1]
     lane = lax.broadcasted_iota(jnp.int32, (W, n), 1)
     row = lax.broadcasted_iota(jnp.int32, (W, n), 0)
-    lane_all = lax.broadcasted_iota(jnp.int32, (n, n), 1)
-
-    def panel(p, carry):
-        rows = pl.ds(pl.multiple_of(p * W, W), W)
-        strip = a_ref[rows, :]
-        cols = [jnp.broadcast_to(strip[:, j : j + 1], (W, n)) for j in range(W)]
-        rest = jnp.where(lane < W, jnp.where(lane == row, 1.0, 0.0), strip)
-        for k in range(W):
-            inv = 1.0 / jnp.broadcast_to(cols[k][k : k + 1, :], (W, n))
-            pivot = row == k
-            weight = cols[k]
-
-            def clear(v):
-                scaled = jnp.broadcast_to(v[k : k + 1, :], (W, n)) * inv
-                return jnp.where(pivot, scaled, v - weight * scaled)
-
-            rest = clear(rest)
-            for j in range(k + 1, W):
-                cols[j] = clear(cols[j])
-        whole = a_ref[...]
-        update = jnp.where(lane_all < W, 0.0, whole)
-        for j in range(W):
-            update = update - whole[:, j : j + 1] * rest[j : j + 1, :]
-        a_ref[...] = pltpu.roll(update, n - W, 1)
-        a_ref[rows, :] = pltpu.roll(rest, n - W, 1)
-        return carry
-
-    lax.fori_loop(0, n // W, panel, 0)
+    cols = [jnp.broadcast_to(strip[:, first + j : first + j + 1], (W, n)) for j in range(W)]
+    turned = pltpu.roll(strip, n - first, 1) if first else strip
+    rest = jnp.where(lane < W, jnp.where(lane == row, 1.0, 0.0), turned)
+    for k in range(W):
+        inv = refine(jnp.broadcast_to(cols[k][k : k + 1, :], (W, n)))
+        pivot = row == k
+        weight = cols[k]
+
+        def clear(v):
+            head = jnp.broadcast_to(v[k : k + 1, :], (W, n))
+            return jnp.where(pivot, head * inv, v - (weight * head) * inv)
+
+        for j in range(k + 1, W):
+            cols[j] = clear(cols[j])
+        rest = clear(rest)
+    return rest
+
+
+def invert_start(a_ref):
+    pivots = pivot_rows(a_ref[0:W, :], 0)
+    return pivots, rank_update(a_ref[W : 2 * W, :], pivots)
+
+
+def apply_rows(a_ref, p, pivots):
+    n = a_ref.shape[0]
+    a_ref[...] = pltpu.roll(rank_update(a_ref[...], pivots), n - W, 1)
+    a_ref[pl.ds(pl.multiple_of(p * W, W), W), :] = pltpu.roll(pivots, n - W, 1)
+
+
+def invert_steps(a_ref, start, stop, state):
+    count = a_ref.shape[0] // W
+
+    def panel(p, state):
+        before, strip = state
+        pivots = pivot_rows(strip, W)
+        apply_rows(a_ref, p - 1, before)
+        follow = lax.rem(p + 1, count)
+        after = a_ref[pl.ds(pl.multiple_of(follow * W, W), W), :]
+        return pivots, rank_update(after, pivots)
+
+    return lax.fori_loop(start, stop, panel, state)
 
 
 def gather_kernel(
     layers, a_ref, blocks_ref, y_ref, shared_ref,
-    sep, mat, diag, mine, near, direct, send_sem, recv_sem, local_sem,
+    sep, lead, mat, diag, mine, near, direct, send_sem, recv_sem, local_sem,
 ):
     leaf = lax.axis_index("leaf")
     layer = lax.axis_index("layer")
@@ -150,46 +177,62 @@
         for slot in (1, 3, 5, 7):
             transfer(slot, q).wait_recv()
 
+    def xor(r):
+        return layer + r - 2 * (
+            lax.rem(layer, 2) * (r % 2) + 2 * lax.rem(layer // 2, 2) * (r // 2)
+        )
+
+    def span(r):
+        return pl.ds(pl.multiple_of(xor(r) * ps, ps), ps)
+
     for load in loads[:layers]:
         load.wait()
     pl.semaphore_wait(barrier, 3)
+    ahead = pltpu.make_async_remote_copy(
+        src_ref=sep.at[0, :, span(0)],
+        dst_ref=lead,
+        send_sem=send_sem.at[0, 0],
+        recv_sem=recv_sem.at[0, 0],
+        device_id=targets[SIBLING],
+        device_id_type=MESH,
+    )
+    ahead.start()
     first(0)
     for load in loads[layers:]:
         load.wait()
     keep = pltpu.make_async_copy(mine, blocks_ref.at[0], local_sem.at[3 * layers])
     keep.start()
-    second(0)
-    first(1)
-    third(0)
-    for q in range(2, chunks + 1):
-        first(q)
-    last(0)
-
-    for r in range(layers):
-        h = layer + r - 2 * (
-            lax.rem(layer, 2) * (r % 2) + 2 * lax.rem(layer // 2, 2) * (r // 2)
-        )
-        mat[pl.ds(pl.multiple_of(h * ps, ps), ps), :] = sep[r] + sep[r + SIBLING]
-
+    ahead.wait_recv()
+    half = ps // W // 2
     for b in range(layers):
-        mid = slice(b * ps, (b + 1) * ps)
-        diag[...] = mat[mid, mid]
-        invert_block(diag)
-        turned = dot32(diag[...], mat[mid, :])
-        mat[mid, :] = turned
+        mid = span(b)
+        diag[...] = sep[0, :, mid] + lead[...] if b == 0 else mat[mid, mid]
+        state = invert_start(diag)
+        state = invert_steps(diag, 1, half, state)
+        if b == 0:
+            second(0)
+            first(1)
+        else:
+            second(b)
+            if b < chunks:
+                first(b + 1)
+        state = invert_steps(diag, half, 2 * half, state)
+        apply_rows(diag, 2 * half - 1, state[0])
+        third(b)
+        if b == 0:
+            last(0)
+            for r in range(layers):
+                mat[span(r), :] = sep[r] + sep[r + SIBLING]
+        mat[mid, :] = dot32(diag[...], mat[mid, :])
         mat[mid, mid] = diag[...]
         turned = mat[mid, :]
         for other in range(layers):
             if other == b:
                 continue
-            rows = slice(other * ps, (other + 1) * ps)
+            rows = span(other)
             weight = mat[rows, mid]
             mat[rows, mid] = jnp.zeros((ps, ps), F32)
             mat[rows, :] = mat[rows, :] - dot32(weight, turned)
-        if b + 1 <= chunks:
-            second(b + 1)
-        if 1 <= b <= chunks:
-            third(b)
     for q in range(layers, chunks + 1):
         third(q)
     last(1)
@@ -203,10 +246,7 @@
     for copy in fetch:
         copy.wait()
     for r in range(layers):
-        h = layer + r - 2 * (
-            lax.rem(layer, 2) * (r % 2) + 2 * lax.rem(layer // 2, 2) * (r // 2)
-        )
-        cols = pl.ds(pl.multiple_of(h * sh, sh), sh)
+        cols = pl.ds(pl.multiple_of(xor(r) * sh, sh), sh)
         far = mine[0:sh, :] if r == 0 else near[r - 1]
         shared_ref[:, cols] = direct[:, cols] - dot32(y_ref[0:sh, :], far, ((1,), (1,)))
     keep.wait()
@@ -215,6 +255,7 @@
     for q in range(chunks + 1):
         for slot in range(1, 8):
             transfer(slot, q).wait_send()
+    ahead.wait_send()
 
 
 def merge_kernel(layers, where_ref, y_ref, block_ref, a_ref, out_ref, wide):
@@ -229,17 +270,25 @@
         wide[:, depth : 2 * depth] = high
         wide[:, 2 * depth : 3 * depth] = low
 
-    high, low = split(block_ref[0])
-    far = jnp.concatenate([high, low, high], axis=1)
+    outer = out_ref.shape[0]
+    slab = a_ref.shape[0]
+    swap = where_ref[0] % 2
+    parts = []
+    for i in range(2):
+        high, low = split(block_ref[jnp.bitwise_xor(swap, i)])
+        parts.append(jnp.concatenate([high, low, high], axis=1))
     product = lax.dot_general(
-        wide[...], far, (((1,), (1,)), ((), ())), preferred_element_type=F32
-    )
-
-    @pl.when(r < layers)
+        wide[...], jnp.concatenate(parts, axis=0), (((1,), (1,)), ((), ())),
+        preferred_element_type=F32,
+    )
+
+    @pl.when(r < layers // 2)
     def _():
-        out_ref[...] = a_ref[ps:, ps:] - product
-
-    @pl.when(r >= layers)
+        for i in range(2):
+            cols = slice(i * outer, (i + 1) * outer)
+            out_ref[:, cols] = a_ref[ps:, i * slab + ps : (i + 1) * slab] - product[:, cols]
+
+    @pl.when(r >= layers // 2)
     def _():
         out_ref[...] = 0.0 - product
 
@@ -268,6 +317,7 @@
         ),
         scratch_shapes=[
             pltpu.VMEM((group, ps, depth), F32),
+            pltpu.VMEM((ps, ps), F32),
             pltpu.VMEM((depth, depth), F32),
             pltpu.VMEM((ps, ps), F32),
             pltpu.VMEM((outer, depth), F32),
@@ -278,31 +328,37 @@
             pltpu.SemaphoreType.DMA((3 * layers + 1,)),
         ],
         compiler_params=pltpu.CompilerParams(
-            collective_id=0, has_side_effects=True, vmem_limit_bytes=40 * 2**20
+            collective_id=0, has_side_effects=True, vmem_limit_bytes=60 * 2**20
         ),
     )(local)
 
     leaf = lax.axis_index("leaf")
     layer = lax.axis_index("layer")
     me = (leaf % 2) * layers + layer
-    order = jnp.bitwise_xor(me, jnp.arange(group, dtype=jnp.int32))
-    slabs = jnp.bitwise_xor(layer, jnp.minimum(jnp.arange(group, dtype=jnp.int32), layers - 1))
-    where = jnp.concatenate([order, slabs]).astype(jnp.int32)
+    where = jnp.full((1,), me, jnp.int32)
     merged = pl.pallas_call(
         functools.partial(merge_kernel, layers),
         out_shape=jax.ShapeDtypeStruct((outer, group * outer), F32),
         grid_spec=pltpu.PrefetchScalarGridSpec(
             num_scalar_prefetch=1,
-            grid=(group,),
+            grid=(group // 2,),
             in_specs=[
                 pl.BlockSpec((outer, depth), lambda r, w: (0, 0)),
-                pl.BlockSpec((1, outer, depth), lambda r, w: (r, 0, 0)),
-                pl.BlockSpec((slab, slab), lambda r, w: (0, w[group + r])),
+                pl.BlockSpec((2, outer, depth), lambda r, w: (r, 0, 0)),
+                pl.BlockSpec(
+                    (slab, 2 * slab),
+                    lambda r, w: (
+                        0,
+                        jnp.bitwise_xor(w[0] % layers // 2, jnp.minimum(r, layers // 2 - 1)),
+                    ),
+                ),
             ],
-            out_specs=pl.BlockSpec((outer, outer), lambda r, w: (0, w[r])),
+            out_specs=pl.BlockSpec(
+                (outer, 2 * outer), lambda r, w: (0, jnp.bitwise_xor(w[0] // 2, r))
+            ),
             scratch_shapes=[pltpu.VMEM((outer, 3 * depth), BF16)],
         ),
-        compiler_params=pltpu.CompilerParams(vmem_limit_bytes=40 * 2**20),
+        compiler_params=pltpu.CompilerParams(vmem_limit_bytes=60 * 2**20),
         cost_estimate=pl.CostEstimate(
             flops=6 * outer * depth * group * outer,
             bytes_accessed=4 * (group * outer * (outer + depth) + slab * width),

time: 71.9 us -> 71.7 us (level)
  local copies, waits for them, and re-layouts: 9.81 us -> 0.01 us
  Pallas kernels: 58.8 us -> 68.5 us
    unnamed x8 -> x2, local copies, waits for them, and re-layouts: 9.81 us -> 0.01 us
    pallas_call x1, Pallas kernels: 50 us -> 59.3 us  [on_device(): pl.pallas_call(functools.partial(gather_kernel, layers), out_shape=(jax.S...]
  transfers between devices with their start and end apart: 1 -> 1, of which waited for: 0 -> 0; matrix products, arithmetic and copies ran while one was open for 0% -> 0% of each run, Pallas kernels for 12% -> 13%
where the time goes in v2:
time: 71.7 us; the launch traced here: 71.5 us
  Pallas kernels  68.5 us (96%)
  starting transfers between devices  1.64 us (2%)
  other arithmetic  0.74 us (1%)
    pallas_call x1, Pallas kernels, on_device(): pl.pallas_call(functools.partial(gather_kernel, layers), out_shape=(jax.S...  59.3 us
    pallas_call x1, Pallas kernels, on_device(): pl.pallas_call(functools.partial(merge_kernel, layers), out_shape=jax.Sha...  9.15 us
    ppermute x1, starting transfers between devices, on_device(): cousin = lax.ppermute(own, 'leaf', [(s, s ^ 2) for s in range(count)])  1.64 us
  transfers between devices with their start and end apart: 1, of which 0 were waited for; matrix products, arithmetic and copies ran while one was open for 0% of the time, Pallas kernels for 13%

profile of v2, /device:TPU:0, one launch (start us, length us, event | category | flops | bytes accessed | tf_op | source)
XLA Modules:
  0.0 71.5 jit_solution(17781270748550766293)
XLA Ops:
  0.6 59.3 %shard_map.30 = (f32[8,384,512]{2,1,0:T(8,128)}, f32[384,512]{1,0:T(8,128)}, f32[128,512]{1,0:T(8,128)}) custom-call(f32[512,2048]{1,0:T(8,128)} %bitcast.5), custom_call_target="tpu_custom_call" | custom-call | tf_op jit(solution)/shard_map/pallas_call | solution.py:305
  60.0 1.6 %collective-permute-start = (f32[128,512]{1,0:T(8,128)}, f32[128,512]{1,0:T(8,128)S(1)}, u32[]{:S(2)}, u32[]{:S(2)}) collective-permute-start(f32[128,512]{1,0:T(8,128)} %get-tuple-element.7), channel_id=1, source_target_pairs={{0,8},{4,12},{8,0},{12,4},{16,24},{20,28},{24,16},{28,20},{1,9},{5... | collective-permute-start | bytes 786440 | tf_op jit(solution)/shard_map/ppermute | solution.py:369
  61.6 0.0 copy-start
  61.6 9.2 %shard_map.31 = f32[384,3072]{1,0:T(8,128)} custom-call(s32[1]{0:T(128)} %bitcast.where_ref, f32[384,512]{1,0:T(8,128)} %get-tuple-element.5.y_ref, f32[8,384,512]{2,1,0:T(8,128)} %get-tuple-element.6.block_ref, f32[512,2048]{1,0:T(8,128)} %bitcast.6), custom_call_target="tpu_custom_call" | custom-call | flops 3623878656 | bytes 15204352 | tf_op jit(solution)/shard_map/pallas_call | solution.py:339
  70.8 0.0 collective-permute-done
  70.8 0.0 copy-done
  70.8 0.7 %add_bitcast_fusion = f32[1,128,512]{2,1,0:T(8,128)} fusion(f32[128,512]{1,0:T(8,128)S(1)} %copy-done, f32[128,512]{1,0:T(8,128)S(1)} %collective-permute-done), kind=kLoop, calls=%fused_computation | loop fusion | flops 65536 | bytes 786432 | tf_op jit(solution)/shard_map/broadcast_in_dim | solution.py:370
Async XLA Ops:
  60.0 10.8 %collective-permute-start = (f32[128,512]{1,0:T(8,128)}, f32[128,512]{1,0:T(8,128)S(1)}, u32[]{:S(2)}, u32[]{:S(2)}) collective-permute-start(f32[128,512]{1,0:T(8,128)} %get-tuple-element.7), channel_id=1, source_target_pairs={{0,8},{4,12},{8,0},{12,4},{16,24},{20,28},{24,16},{28,20},{1,9},{5... | collective-permute-start | bytes 786440 | tf_op jit(solution)/shard_map/ppermute | solution.py:369
  61.6 9.2 %copy-start = (f32[128,512]{1,0:T(8,128)S(1)}, f32[128,512]{1,0:T(8,128)}, u32[]{:S(2)}) copy-start(f32[128,512]{1,0:T(8,128)} %get-tuple-element.7) | copy-start | bytes 786436

commit v3 on v2

--- a/solution.py
+++ b/solution.py
@@ -47,16 +47,29 @@
     cols = [jnp.broadcast_to(strip[:, first + j : first + j + 1], (W, n)) for j in range(W)]
     turned = pltpu.roll(strip, n - first, 1) if first else strip
     rest = jnp.where(lane < W, jnp.where(lane == row, 1.0, 0.0), turned)
-    for k in range(W):
-        inv = refine(jnp.broadcast_to(cols[k][k : k + 1, :], (W, n)))
-        pivot = row == k
-        weight = cols[k]
+
+    def spread(v, k):
+        return jnp.broadcast_to(v[k : k + 1, :], (W, n))
+
+    scale = [pl.reciprocal(spread(cols[k], k), approx=True) for k in range(W)]
+    for k in range(0, W, 2):
+        ua, uc = scale[k], scale[k + 1]
+        a, b, c = spread(cols[k], k), spread(cols[k], k + 1), spread(cols[k + 1], k + 1)
+        au, cu, bu = a * ua, c * uc, b * ua
+        inv = refine(au * cu - bu * (b * uc))
+        first_first, second_second, cross = cu * ua, au * uc, bu * uc
+        w1, w2 = cols[k], cols[k + 1]
 
         def clear(v):
-            head = jnp.broadcast_to(v[k : k + 1, :], (W, n))
-            return jnp.where(pivot, head * inv, v - (weight * head) * inv)
-
-        for j in range(k + 1, W):
+            v1, v2 = spread(v, k), spread(v, k + 1)
+            n1 = first_first * v1 - cross * v2
+            n2 = second_second * v2 - cross * v1
+            q = w1 * n1 + w2 * n2
+            left = jnp.where(row == k, 0.0, jnp.where(row == k + 1, 0.0, v))
+            q = jnp.where(row == k, -n1, jnp.where(row == k + 1, -n2, q))
+            return left - q * inv
+
+        for j in range(k + 2, W):
             cols[j] = clear(cols[j])
         rest = clear(rest)
     return rest
@@ -69,8 +82,12 @@
 
 def apply_rows(a_ref, p, pivots):
     n = a_ref.shape[0]
-    a_ref[...] = pltpu.roll(rank_update(a_ref[...], pivots), n - W, 1)
-    a_ref[pl.ds(pl.multiple_of(p * W, W), W), :] = pltpu.roll(pivots, n - W, 1)
+    turned = pltpu.roll(pivots, n - W, 1)
+    lane = lax.broadcasted_iota(jnp.int32, (n - W, n), 1)
+    row = lax.broadcasted_iota(jnp.int32, (n - W, n), 0)
+    step = jnp.concatenate([-turned, jnp.where(lane == row, 1.0, 0.0)], axis=0)
+    a_ref[...] = dot32(a_ref[...], step)
+    a_ref[pl.ds(pl.multiple_of(p * W, W), W), :] = turned
 
 
 def invert_steps(a_ref, start, stop, state):
@@ -88,8 +105,8 @@
 
 
 def gather_kernel(
-    layers, a_ref, blocks_ref, y_ref, shared_ref,
-    sep, lead, mat, diag, mine, near, direct, send_sem, recv_sem, local_sem,
+    layers, a_ref, out_ref, shared_ref,
+    sep, lead, mat, diag, mine, direct, blocks_ref, y_ref, wide, result, own, cousin, send_sem, recv_sem, local_sem,
 ):
     leaf = lax.axis_index("leaf")
     layer = lax.axis_index("layer")
@@ -114,7 +131,8 @@
     )
 
     barrier = pltpu.get_barrier_semaphore()
-    for target in targets.values():
+    relative = (flip(leaf, 2), layer)
+    for target in (*targets.values(), relative):
         pl.semaphore_signal(barrier, inc=1, device_id=target, device_id_type=MESH)
 
     loads = []
@@ -130,8 +148,8 @@
             a_ref.at[pl.ds(ps, outer), cols], mine.at[:, into], local_sem.at[layers + h]))
     for h in range(layers):
         loads.append(pltpu.make_async_copy(
-            a_ref.at[pl.ds(ps, sh), pl.ds(h * slab + ps, sh)],
-            direct.at[:, pl.ds(h * sh, sh)], local_sem.at[2 * layers + h]))
+            a_ref.at[pl.ds(ps, outer), pl.ds(h * slab + ps, outer)],
+            direct.at[:, pl.ds(h * outer, outer)], local_sem.at[2 * layers + h]))
     for load in loads:
         load.start()
 
@@ -187,7 +205,7 @@
 
     for load in loads[:layers]:
         load.wait()
-    pl.semaphore_wait(barrier, 3)
+    pl.semaphore_wait(barrier, 4)
     ahead = pltpu.make_async_remote_copy(
         src_ref=sep.at[0, :, span(0)],
         dst_ref=lead,
@@ -198,7 +216,7 @@
     )
     ahead.start()
     first(0)
-    for load in loads[layers:]:
+    for load in loads[layers : 2 * layers]:
         load.wait()
     keep = pltpu.make_async_copy(mine, blocks_ref.at[0], local_sem.at[3 * layers])
     keep.start()
@@ -209,13 +227,10 @@
         diag[...] = sep[0, :, mid] + lead[...] if b == 0 else mat[mid, mid]
         state = invert_start(diag)
         state = invert_steps(diag, 1, half, state)
+        second(b)
         if b == 0:
-            second(0)
-            first(1)
-        else:
-            second(b)
-            if b < chunks:
-                first(b + 1)
+            for q in range(1, chunks + 1):
+                first(q)
         state = invert_steps(diag, half, 2 * half, state)
         apply_rows(diag, 2 * half - 1, state[0])
         third(b)
@@ -235,62 +250,67 @@
             mat[rows, :] = mat[rows, :] - dot32(weight, turned)
     for q in range(layers, chunks + 1):
         third(q)
+    y_ref[...] = dot32(mine[...], mat[...])
+    depth = y_ref.shape[1]
+    high, low = split(y_ref[...])
+    wide[:, 0:depth] = high
+    wide[:, depth : 2 * depth] = high
+    wide[:, 2 * depth : 3 * depth] = low
+    for load in loads[2 * layers :]:
+        load.wait()
     last(1)
-    fetch = [
-        pltpu.make_async_copy(blocks_ref.at[r, pl.ds(0, sh), :], near.at[r - 1], local_sem.at[r])
-        for r in range(1, layers)
-    ]
-    for copy in fetch:
-        copy.start()
-    y_ref[...] = dot32(mine[...], mat[...])
-    for copy in fetch:
-        copy.wait()
     for r in range(layers):
         cols = pl.ds(pl.multiple_of(xor(r) * sh, sh), sh)
-        far = mine[0:sh, :] if r == 0 else near[r - 1]
-        shared_ref[:, cols] = direct[:, cols] - dot32(y_ref[0:sh, :], far, ((1,), (1,)))
+        from_cols = pl.ds(pl.multiple_of(xor(r) * outer, sh), sh)
+        far = mine[0:sh, :] if r == 0 else blocks_ref[r, 0:sh, :]
+        own[:, cols] = direct[0:sh, from_cols] - dot32(y_ref[0:sh, :], far, ((1,), (1,)))
+    swap = pltpu.make_async_remote_copy(
+        src_ref=own,
+        dst_ref=cousin,
+        send_sem=send_sem.at[0, 1],
+        recv_sem=recv_sem.at[0, 1],
+        device_id=relative,
+        device_id_type=MESH,
+    )
+    swap.start()
     keep.wait()
-    for q in range(2, chunks + 1):
-        last(q)
+    pair = 2 * outer
+    writes = []
+    for t in range(layers):
+        for q in range(2, chunks + 1):
+            transfer(2 * t + 1, q).wait_recv()
+        near = t < layers // 2
+        place_in = xor(2 * (t % (layers // 2))) // 2
+        parity = lax.rem(leaf, 2)
+        side = parity if near else 1 - parity
+        parts = []
+        for i in range(2):
+            slot = 2 * t + (core if i == 0 else 1 - core)
+            high, low = split(blocks_ref[slot])
+            parts.append(jnp.concatenate([high, low, high], axis=1))
+        product = lax.dot_general(
+            wide[...], jnp.concatenate(parts, axis=0), (((1,), (1,)), ((), ())),
+            preferred_element_type=F32,
+        )
+        if near:
+            product = direct[:, pl.ds(pl.multiple_of(place_in * pair, sh), pair)] - product
+        else:
+            product = 0.0 - product
+        result[t] = product
+        to = (side * (layers // 2) + place_in) * pair
+        write = pltpu.make_async_copy(
+            result.at[t], out_ref.at[:, pl.ds(pl.multiple_of(to, sh), pair)], local_sem.at[t]
+        )
+        write.start()
+        writes.append(write)
+    swap.wait()
+    shared_ref[...] = own[...] + cousin[...]
+    for write in writes:
+        write.wait()
     for q in range(chunks + 1):
         for slot in range(1, 8):
             transfer(slot, q).wait_send()
     ahead.wait_send()
-
-
-def merge_kernel(layers, where_ref, y_ref, block_ref, a_ref, out_ref, wide):
-    r = pl.program_id(0)
-    depth = y_ref.shape[1]
-    ps = a_ref.shape[0] - out_ref.shape[0]
-
-    @pl.when(r == 0)
-    def _():
-        high, low = split(y_ref[...])
-        wide[:, 0:depth] = high
-        wide[:, depth : 2 * depth] = high
-        wide[:, 2 * depth : 3 * depth] = low
-
-    outer = out_ref.shape[0]
-    slab = a_ref.shape[0]
-    swap = where_ref[0] % 2
-    parts = []
-    for i in range(2):
-        high, low = split(block_ref[jnp.bitwise_xor(swap, i)])
-        parts.append(jnp.concatenate([high, low, high], axis=1))
-    product = lax.dot_general(
-        wide[...], jnp.concatenate(parts, axis=0), (((1,), (1,)), ((), ())),
-        preferred_element_type=F32,
-    )
-
-    @pl.when(r < layers // 2)
-    def _():
-        for i in range(2):
-            cols = slice(i * outer, (i + 1) * outer)
-            out_ref[:, cols] = a_ref[ps:, i * slab + ps : (i + 1) * slab] - product[:, cols]
-
-    @pl.when(r >= layers // 2)
-    def _():
-        out_ref[...] = 0.0 - product
 
 
 def on_device(layers, schur_blocks):
@@ -302,17 +322,15 @@
     sh = ps
     group = 2 * layers
     chunks = outer // ps
-    blocks, y, own = pl.pallas_call(
+    merged, cousin_sum = pl.pallas_call(
         functools.partial(gather_kernel, layers),
         out_shape=(
-            jax.ShapeDtypeStruct((group, outer, depth), F32),
-            jax.ShapeDtypeStruct((outer, depth), F32),
+            jax.ShapeDtypeStruct((outer, group * outer), F32),
             jax.ShapeDtypeStruct((sh, layers * sh), F32),
         ),
         in_specs=[pl.BlockSpec(memory_space=pl.ANY)],
         out_specs=(
             pl.BlockSpec(memory_space=pl.ANY),
-            pl.BlockSpec(memory_space=pltpu.VMEM),
             pl.BlockSpec(memory_space=pltpu.VMEM),
         ),
         scratch_shapes=[
@@ -321,7 +339,12 @@
             pltpu.VMEM((depth, depth), F32),
             pltpu.VMEM((ps, ps), F32),
             pltpu.VMEM((outer, depth), F32),
-            pltpu.VMEM((layers - 1, sh, depth), F32),
+            pltpu.VMEM((outer, layers * outer), F32),
+            pltpu.VMEM((group, outer, depth), F32),
+            pltpu.VMEM((outer, depth), F32),
+            pltpu.VMEM((outer, 3 * depth), BF16),
+            pltpu.VMEM((layers, outer, 2 * outer), F32),
+            pltpu.VMEM((sh, layers * sh), F32),
             pltpu.VMEM((sh, layers * sh), F32),
             pltpu.SemaphoreType.DMA((group, chunks + 1)),
             pltpu.SemaphoreType.DMA((group, chunks + 1)),
@@ -331,43 +354,7 @@
             collective_id=0, has_side_effects=True, vmem_limit_bytes=60 * 2**20
         ),
     )(local)
-
-    leaf = lax.axis_index("leaf")
-    layer = lax.axis_index("layer")
-    me = (leaf % 2) * layers + layer
-    where = jnp.full((1,), me, jnp.int32)
-    merged = pl.pallas_call(
-        functools.partial(merge_kernel, layers),
-        out_shape=jax.ShapeDtypeStruct((outer, group * outer), F32),
-        grid_spec=pltpu.PrefetchScalarGridSpec(
-            num_scalar_prefetch=1,
-            grid=(group // 2,),
-            in_specs=[
-                pl.BlockSpec((outer, depth), lambda r, w: (0, 0)),
-                pl.BlockSpec((2, outer, depth), lambda r, w: (r, 0, 0)),
-                pl.BlockSpec(
-                    (slab, 2 * slab),
-                    lambda r, w: (
-                        0,
-                        jnp.bitwise_xor(w[0] % layers // 2, jnp.minimum(r, layers // 2 - 1)),
-                    ),
-                ),
-            ],
-            out_specs=pl.BlockSpec(
-                (outer, 2 * outer), lambda r, w: (0, jnp.bitwise_xor(w[0] // 2, r))
-            ),
-            scratch_shapes=[pltpu.VMEM((outer, 3 * depth), BF16)],
-        ),
-        compiler_params=pltpu.CompilerParams(vmem_limit_bytes=60 * 2**20),
-        cost_estimate=pl.CostEstimate(
-            flops=6 * outer * depth * group * outer,
-            bytes_accessed=4 * (group * outer * (outer + depth) + slab * width),
-            transcendentals=0,
-        ),
-    )(where, y, blocks, local)
-    count = lax.axis_size("leaf")
-    cousin = lax.ppermute(own, "leaf", [(s, s ^ 2) for s in range(count)])
-    return (merged[None], (own + cousin)[None])
+    return (merged[None], cousin_sum[None])
 
 
 def solution(mesh):

time: 71.7 us -> 73.8 us (1.029)
  local copies, waits for them, and re-layouts: 0.01 us -> 5.8 us
  starting transfers between devices: 1.64 us -> 0 us
  Pallas kernels: 68.5 us -> 67.2 us
  other arithmetic: 0.74 us -> 0 us
    pallas_call x1 -> x0, Pallas kernels: 9.15 us -> none  [on_device(): pl.pallas_call(functools.partial(merge_kernel, layers), out_shape=jax.Sha...]
    pallas_call x1, Pallas kernels: 59.3 us -> 67.2 us  [on_device(): pl.pallas_call(functools.partial(gather_kernel, layers), out_shape=(jax.S...]
    unnamed x2 -> x4, local copies, waits for them, and re-layouts: 0.01 us -> 5.8 us
    ppermute x1 -> x0, starting transfers between devices: 1.64 us -> none  [on_device(): cousin = lax.ppermute(own, 'leaf', [(s, s ^ 2) for s in range(count)])]
    broadcast_in_dim x1 -> x0, other arithmetic: 0.74 us -> none  [on_device(): return (merged[None], (own + cousin)[None])]
  transfers between devices with their start and end apart: 1 -> 0, of which waited for: 0 -> 0; matrix products, arithmetic and copies ran while one was open for 0% -> 0% of each run, Pallas kernels for 13% -> 0%
where the time goes in v3:
time: 73.8 us; the launch traced here: 73.6 us
  Pallas kernels  67.2 us (91%)
  local copies, waits for them, and re-layouts  5.8 us (8%)
    pallas_call x1, Pallas kernels, on_device(): pl.pallas_call(functools.partial(gather_kernel, layers), out_shape=(jax.S...  67.2 us
    unnamed x4, local copies, waits for them, and re-layouts  5.8 us

profile of v3, /device:TPU:0, one launch (start us, length us, event | category | flops | bytes accessed | tf_op | source)
XLA Modules:
  0.0 73.6 jit_solution(9909768685417990144)
XLA Ops:
  0.6 67.2 %shard_map.30 = (f32[384,3072]{1,0:T(8,128)}, f32[128,512]{1,0:T(8,128)}) custom-call(f32[512,2048]{1,0:T(8,128)} %bitcast.4), custom_call_target="tpu_custom_call" | custom-call | tf_op jit(solution)/shard_map/pallas_call | solution.py:325
  67.8 0.0 copy-start
  67.8 5.1 %copy.5 = f32[1,384,3072]{2,1,0:T(8,128)} copy(f32[1,384,3072]{2,1,0:T(8,128)} %bitcast.3) | data formatting | bytes 9437184
  72.9 0.0 copy-done
  72.9 0.7 copy.6
Async XLA Ops:
  67.8 5.1 %copy-start = (f32[128,512]{1,0:T(8,128)S(1)}, f32[128,512]{1,0:T(8,128)}, u32[]{:S(2)}) copy-start(f32[128,512]{1,0:T(8,128)} %get-tuple-element.5) | copy-start | bytes 786436
